TPU v7x, 32 devices: a whole 2x2x4 slice. The times are simulated.
32 devices in a mesh: ctx: 16 (over z, x, core), head: 2 (over y).
Axes of the slice: x: 2, y: 2, z: 4, core: 2. Of those that a mesh axis runs over, the one named last changes fastest.
Arguments:
- queries: bfloat16 [16384, 4096], P('ctx', 'head')
- keys: bfloat16 [16384, 4096], P('ctx', 'head'), may hold values from -5 to 5
- values: bfloat16 [16384, 4096], P('ctx', 'head')
- log_decay: float32 [16384, 32], P('ctx', 'head'), as said below
- gate: bfloat16 [16384, 4096], P('ctx', 'head'), may hold values from -6 to 6
- norm_gain: float32 [4096], replicated, may hold values from 0.1 to 1.9
Outputs:
- output: bfloat16 [16384, 4096], P(('ctx', 'head'))
Inputs may be any that keep to these rules, and one draw needn't show every extreme that they name: `log_decay`: every entry is at most 0.
All inputs are finite; a program needn't handle non-finite values.
Results may differ from a plain program's by a relative error of at most 0.0085.
Values may be sent and summed in bfloat16 or wider, within the bound.
A program may use at most 128 MiB of HBM per device.

v0:
```python
import jax
import jax.numpy as jnp
from jax import lax
from jax.sharding import PartitionSpec as P

eps_norm = 1e-05


def carried_in(value, axis, join, neutral):
    count, mine = (lax.axis_size(axis), lax.axis_index(axis))
    pieces = jax.tree.map(lambda part: lax.all_gather(part, axis), value)
    subtotal = jax.tree.map(
        lambda part, zero: jnp.full_like(part, 0) + jnp.asarray(zero, part.dtype), value, neutral
    )

    def step(position, subtotal):
        longer = join(subtotal, jax.tree.map(lambda part: part[position], pieces))
        return jax.tree.map(lambda new, old: jnp.where(position < mine, new, old), longer, subtotal)

    return lax.fori_loop(0, count - 1, step, subtotal)


def head_block(qh, kh, vh, ch):
    count = qh.shape[0]
    target_index = jnp.arange(count)
    causal = target_index[:, None] >= target_index[None, :]
    scores = jnp.dot(qh, kh.T, preferred_element_type=jnp.float32)
    spread = jnp.where(causal, ch[:, None] - ch[None, :], 0.0)
    weights = (scores * jnp.where(causal, jnp.exp(spread), 0.0)).astype(jnp.bfloat16)
    inner = jnp.dot(weights, vh, preferred_element_type=jnp.float32)
    keyed = kh.astype(jnp.float32) * jnp.exp(ch[-1] - ch)[:, None]
    state = jnp.dot(keyed.T, vh.astype(jnp.float32), precision=lax.Precision.HIGHEST)
    return (inner, state)


def split_heads(block, heads):
    count = block.shape[0]
    return block.reshape(count, heads, block.shape[1] // heads).transpose(1, 0, 2)


def local_block(queries, keys, values, log_decay):
    heads = log_decay.shape[1]
    cum = jnp.cumsum(log_decay, axis=0)
    inner, state = lax.map(
        lambda parts: head_block(parts[0], parts[1], parts[2], parts[3]),
        (split_heads(queries, heads), split_heads(keys, heads), split_heads(values, heads), cum.T),
    )
    return (cum, inner, state)


def join_block(queries, cum, inner, carried):
    heads = cum.shape[1]
    count = queries.shape[0]
    qfloat = split_heads(queries, heads).astype(jnp.float32)
    across = jnp.einsum("hcd,hde->hce", qfloat, carried, precision=lax.Precision.HIGHEST)
    total = inner + jnp.exp(cum).T[:, :, None] * across
    return total.transpose(1, 0, 2).reshape(count, queries.shape[1]).astype(jnp.bfloat16)


def chain(earlier, later):
    return (earlier[0] * later[0], later[0][:, None, None] * earlier[1] + later[1])


def body(queries, keys, values, log_decay, gate, norm_gain):
    cum, inner, state = local_block(queries, keys, values, log_decay)
    heads = log_decay.shape[1]
    size = state.shape[1]
    totals = cum[-1]
    identity_pair = (jnp.ones((heads,), jnp.float32), jnp.zeros((heads, size, size), jnp.float32))
    passed = carried_in((jnp.exp(totals), state), "ctx", chain, identity_pair)
    carried = passed[1]
    attended = join_block(queries, cum, inner, carried)
    width = queries.shape[1]
    shade = attended.astype(jnp.float32)
    sums = lax.psum(jnp.sum(shade * shade, axis=1), "head")
    columns = width * lax.axis_size("head")
    scale = lax.rsqrt(sums / columns + eps_norm)[:, None]
    gain = lax.dynamic_slice_in_dim(norm_gain, lax.axis_index("head") * width, width, 0)
    shaped = (shade * scale * gain * jax.nn.sigmoid(gate.astype(jnp.float32))).astype(jnp.bfloat16)
    return lax.all_to_all(shaped, "head", split_axis=0, concat_axis=1, tiled=True)


def solution(mesh):
    in_specs = (
        P("ctx", "head"),
        P("ctx", "head"),
        P("ctx", "head"),
        P("ctx", "head"),
        P("ctx", "head"),
        P(),
    )
    out_specs = P(("ctx", "head"), None)
    return jax.shard_map(body, mesh=mesh, in_specs=in_specs, out_specs=out_specs, check_vma=False)
```

profile of v0, /device:TPU:26, one launch (start us, length us, event | category | flops | bytes accessed | tf_op | source)
XLA Modules:
  0.0 408.3 jit_solution(2797235634207529316)
XLA Ops:
  7.4 4.5 %reduce-window.6 = f32[16,8,128]{2,1,0:T(8,128)S(1)} reduce-window(f32[16,8,128]{2,1,0:T(8,128)S(1)} %bitcast.112, f32[]{:T(128)} %constant.59.clone.1), window={size=1x1x128 pad=0_0x0_0x127_0}, to_apply=%region_0.0 | reduce-window | flops 2080768 | bytes 131076 | tf_op jit(solution)/shard_map/reduce-window
  12.4 6.4 %copy.38 = bf16[1024,2048]{0,1:T(8,128)(2,1)} copy(bf16[1024,2048]{1,0:T(8,128)(2,1)} %param.10) | data formatting | bytes 8388608 | tf_op args[0]
  18.8 6.4 %copy.39 = bf16[1024,2048]{0,1:T(8,128)(2,1)} copy(bf16[1024,2048]{1,0:T(8,128)(2,1)} %param.11) | data formatting | bytes 8388608 | tf_op args[1]
  25.2 6.4 %copy.42 = bf16[1024,2048]{0,1:T(8,128)(2,1)} copy(bf16[1024,2048]{1,0:T(8,128)(2,1)} %param.12) | data formatting | bytes 8388608 | tf_op args[2]
  31.6 126.9 %while.26 = (s32[]{:T(128)}, f32[16,1024,128]{1,2,0:T(8,128)}, f32[16,128,128]{2,1,0:T(8,128)}, bf16[16,1024,128]{1,2,0:T(8,128)(2,1)}, bf16[16,1024,128]{1,2,0:...) while((s32[]{:T(128)}, f32[16,1024,128]{1,2,0:T(8,128)}, ...), condition=%wide.region_3.4_spmd, body=%wide.region_2.3_spmd.sunk | while | flops 744752128 | bytes 2981001 | solution.py:44
  33.9 2.3 fusion.44
  36.2 3.3 fusion.43
  41.8 2.3 fusion.44
  44.1 3.3 fusion.43
  49.7 2.3 fusion.44
  52.0 3.3 fusion.43
  57.7 2.3 fusion.44
  60.0 3.3 fusion.43
  65.6 2.3 fusion.44
  67.9 3.3 fusion.43
  73.5 2.3 fusion.44
  75.8 3.3 fusion.43
  81.5 2.3 fusion.44
  83.8 3.3 fusion.43
  89.4 2.3 fusion.44
  91.7 3.3 fusion.43
  97.3 2.3 fusion.44
  99.6 3.3 fusion.43
  105.2 2.3 fusion.44
  107.6 3.3 fusion.43
  113.2 2.3 fusion.44
  115.5 3.3 fusion.43
  121.1 2.3 fusion.44
  123.4 3.3 fusion.43
  129.0 2.3 fusion.44
  131.4 3.3 fusion.43
  137.0 2.3 fusion.44
  139.3 3.3 fusion.43
  144.9 2.3 fusion.44
  147.2 3.3 fusion.43
  152.8 2.3 fusion.44
  155.2 3.3 fusion.43
  158.7 16.5 %all-gather.1 = f32[16,1,16]{2,1,0:T(1,128)S(1)} all-gather(f32[1,1,16]{2,1,0:T(1,128)S(1)} %bitcast.118), channel_id=1, replica_groups=mesh['ctx'=16,'head'=2] {'ctx'}, dimensions={0}, use_global_device_ids=true | all-gather | bytes 1088 | tf_op jit(solution)/shard_map/all_gather | solution.py:11
  175.2 108.3 %all-gather.4.cloned.1.call-done = f32[256,128,128]{2,1,0:T(8,128)} async-done(((f32[16,128,128]{2,1,0:T(8,128)}), f32[256,128,128]{2,1,0:T(8,128)}) %all-gather.4.cloned.1.call-update) | async-done | bytes 16777232 | tf_op jit(solution)/shard_map/all_gather | solution.py:11
  283.5 22.4 %while.27 = (s32[]{:T(128)}, f32[16,128,128]{2,1,0:T(8,128)S(1)}, s32[]{:T(128)}, f32[16,16]{1,0:T(8,128)S(1)}, f32[16,16,128,128]{3,2,1,0:T(8,128)}, /*index=5*/s32[]{:T(128)}, s32[]{:T(128)}) while((s32[]{:T(128)}, f32[16,128,128]{2,1,0:T(8,128)S(1)}, s32[]{:T(128)}, f32[16,16]{1,0:T(8,128)S(1)}, f32[16,16,128,128]{3,2,1,0:T(8,128)}, ...), condition=%wide.region_5.6_spmd.clone, body=%wide.region_4.5_spmd.clone.sunk | while | flops 1048580 | bytes 3146025 | solution.py:20
  286.5 1.5 fusion.45
  306.0 12.2 %multiply_reduce_fusion = (f32[1024]{0:T(1024)S(1)}, f32[16,1024,128]{1,2,0:T(8,128)}) fusion(f32[16,1024,128]{1,2,0:T(8,128)} %get-tuple-element.137, f32[16,128,128]{2,1,0:T(8,128)S(1)} %get-tuple-element.139, bf16[16,1024,128]{1,2,0:T(8,128)(2,1)} %get-tuple-element.333, f32[16,1024]{1,0:T(8,128)S(1)} %fusion.27), kind=kOutput, calls=%fused_computation.30 | convolution fusion | flops 3233807360 | bytes 22089728 | tf_op jit(solution)/shard_map/hcd,hde->hce/dot_general | solution.py:55
  318.2 9.1 %copy.49 = f32[1024,2048]{1,0:T(8,128)} copy(f32[1024,2048]{0,1:T(8,128)} %bitcast.101) | data formatting | bytes 16777216 | tf_op jit(solution)/shard_map/convert_element_type | solution.py:74
  327.3 4.9 %psum.7 = f32[1024]{0:T(1024)S(1)} all-reduce(f32[1024]{0:T(1024)S(1)} %get-tuple-element.205), channel_id=1, replica_groups=mesh['ctx'=16,'head'=2] {'head'}, use_global_device_ids=true, to_apply=%region_7.8 | all-reduce | flops 1024 | bytes 8192 | tf_op jit(solution)/shard_map/psum | solution.py:75
  332.3 6.0 %multiply_convert_fusion.1 = bf16[1024,2048]{1,0:T(8,128)(2,1)S(1)} fusion(bf16[1024,2048]{1,0:T(8,128)(2,1)} %param.14, f32[1024,2048]{1,0:T(8,128)} %copy.49, f32[2048]{0:T(1024)S(1)} %dynamic-slice-done, f32[1024]{0:T(1024)S(1)} %add_rsqrt_fusion), kind=kLoop, calls=%fused_computation.29 | loop fusion | flops 16777216 | bytes 16789504 | tf_op jit(solution)/shard_map/convert_element_type | solution.py:79
  338.3 50.6 %all_to_all.19 = bf16[2,512,2048]{2,1,0:T(8,128)(2,1)} all-to-all(bf16[2,512,2048]{2,1,0:T(8,128)(2,1)S(1)} %bitcast.104), channel_id=1, replica_groups=mesh['ctx'=16,'head'=2] {'head'}, dimensions={0} | all-to-all | bytes 8388608 | tf_op jit(solution)/shard_map/all_to_all | solution.py:80
  388.9 6.2 %copy.50 = bf16[2,512,2048]{1,2,0:T(8,128)(2,1)} copy(bf16[2,512,2048]{2,1,0:T(8,128)(2,1)} %all_to_all.19) | data formatting | bytes 8388608 | tf_op jit(solution)/shard_map/all_to_all | solution.py:80
  395.1 6.3 %copy.51 = bf16[512,4096]{1,0:T(8,128)(2,1)} copy(bf16[512,4096]{0,1:T(8,128)(2,1)} %bitcast.102) | data formatting | bytes 8388608 | tf_op jit(solution)/shard_map/all_to_all | solution.py:80
  (127 shorter events, 58.6 us)
Async XLA Ops:
  6.5 277.0 %all-gather.4.cloned.1.call-start = ((), (), s32[]{:S(2)}) async-start(), calls=%async_computation.1 | async-start | bytes 17825792 | tf_op jit(solution)/shard_map/all_gather | solution.py:11
  318.2 14.1 %dynamic-slice-start = ((f32[4096]{0:T(1024)}, s32[]{:T(128)}), f32[2048]{0:T(1024)S(1)}, s32[]{:S(2)}) async-start(f32[4096]{0:T(1024)} %param.15, s32[]{:T(128)} %select_n.32), calls=%async_computation.2 | async-start | bytes 16896 | tf_op jit(solution)/shard_map/dynamic_slice | solution.py:78
Sparse Core Ops, SparseCore 0:
  158.6 124.8 all-gather.3
where the time goes:
time: 416 us; the launch traced here: 408 us
  waiting for transfers between devices  108 us (26%)
  matrix products  102 us (25%)
  blocking collectives  72 us (17%)
  local copies, waits for them, and re-layouts  69.8 us (17%)
  other arithmetic  41.7 us (10%)
  between operations  13.5 us (3%)
    all_gather x1, waiting for transfers between devices, carried_in(): pieces = jax.tree.map(lambda part: lax.all_gather(part, axis), value)  108 us
    dot_general x16, matrix products, head_block(): inner = jnp.dot(weights, vh, preferred_element_type=jnp.float32)  53 us
    all_to_all x1, blocking collectives, body(): lax.all_to_all(shaped, 'head', split_axis=0, concat_axis=1, tiled=True)  50.6 us
    dot_general x16, matrix products, head_block(): jnp.dot(keyed.T, vh.astype(jnp.float32), precision=lax.Precision.HIGHEST)  37.1 us
    select_n x15, other arithmetic, step(): jnp.where(position < mine, new, old)  21.9 us
    unnamed x5, local copies, waits for them, and re-layouts  20.1 us
    dynamic_slice x48, local copies, waits for them, and re-layouts, local_block(): lax.map(lambda parts: head_block(parts[0], parts[1], parts[2], parts[3]),...  18.4 us
    all_gather x1, blocking collectives, carried_in(): pieces = jax.tree.map(lambda part: lax.all_gather(part, axis), value)  16.5 us
  transfers between devices with their start and end apart: 1, of which 1 were waited for; matrix products, arithmetic and copies ran while one was open for 0% of the time, Pallas kernels for 0%

commit v1 on v0

v1 whole, which is shorter than its diff:
```python
import functools

import jax
import jax.numpy as jnp
from jax import lax
from jax.experimental import pallas as pl
from jax.experimental.pallas import tpu as pltpu
from jax.sharding import PartitionSpec as P

eps_norm = 1e-05
HD = 128
SUB = 256
f32 = jnp.float32
bf16 = jnp.bfloat16
MESH = pl.DeviceIdType.MESH


def dot(a, b, dims, precision=None):
    return lax.dot_general(a, b, (dims, ((), ())), precision=precision, preferred_element_type=f32)


def kernel(
    n_ctx, n_head, group, heads, ahead, fetch,
    q_hbm, k_hbm, v_hbm, g_hbm, ld_ref, gain_ref,
    out_hbm, ssq_ref,
    q_v, k_v, v_v, g_v, u_v, clt, clc, dlast, sst, mine, gath, tsend, tgath, ein, eout, acc, rows_own, rows_in,
    load_sem, gs_sem, gr_sem, ts_sem, tr_sem, es_sem, er_sem, ys_sem, yr_sem, own_sem, ss_sem, sr_sem,
):
    count = ld_ref.shape[1]
    subs = count // SUB
    rows = count // n_head
    planes = n_ctx // group
    ci = lax.axis_index("ctx")
    hi = lax.axis_index("head")
    plane = ci // group
    r = lax.rem(ci, group)
    base = plane * group
    first = plane == 0
    last = plane == planes - 1

    def peer(off):
        return base + lax.rem(r + off, group)

    def hpeer(off):
        return lax.rem(hi + off, n_head)

    barrier = pltpu.get_barrier_semaphore()

    def greet(**where):
        pl.semaphore_signal(barrier, inc=1, device_id=where, device_id_type=MESH)

    for off in range(1, group):
        greet(ctx=peer(off))
    for off in range(1, n_head):
        greet(head=hpeer(off))

    @pl.when(jnp.logical_not(first))
    def _():
        greet(ctx=ci - group)

    @pl.when(jnp.logical_not(last))
    def _():
        greet(ctx=ci + group)

    def cols(h):
        return pl.ds(pl.multiple_of(h * HD, HD), HD)

    def load(h, which):
        src, dst = ((k_hbm, k_v), (v_hbm, v_v), (q_hbm, q_v), (g_hbm, g_v))[which]
        return pltpu.make_async_copy(src.at[:, cols(h)], dst.at[:, cols(h)], load_sem.at[which, h])

    for h in range(fetch):
        load(h, 0).start()
        load(h, 1).start()
    for h in range(fetch):
        load(h, 2).start()
        load(h, 3).start()

    up = (
        lax.broadcasted_iota(jnp.int32, (SUB, SUB), 0) <= lax.broadcasted_iota(jnp.int32, (SUB, SUB), 1)
    ).astype(f32)
    total = jnp.zeros((heads, 1), f32)
    tall = []
    for s in range(subs):
        cl = dot(ld_ref[:, s * SUB:(s + 1) * SUB], up, ((1,), (0,)), lax.Precision.HIGHEST)
        clt[:, s * SUB:(s + 1) * SUB] = cl
        tall.append(jnp.transpose(cl))
        end = cl[:, SUB - 1:SUB]
        dlast[s] = jnp.broadcast_to(end, (heads, HD))
        total = total + end
    tsend[...] = jnp.broadcast_to(total, (heads, HD))
    acc[...] = jnp.zeros_like(acc)

    def tcopy(off):
        return pltpu.make_async_remote_copy(
            src_ref=tsend, dst_ref=tgath.at[r], send_sem=ts_sem.at[off], recv_sem=tr_sem.at[r],
            device_id={"ctx": peer(off)}, device_id_type=MESH)

    def gcopy(h, off):
        return pltpu.make_async_remote_copy(
            src_ref=mine.at[h], dst_ref=gath.at[r, h], send_sem=gs_sem.at[h, off], recv_sem=gr_sem.at[h, r],
            device_id={"ctx": peer(off)}, device_id_type=MESH)

    def grecv(h, slot):
        return pltpu.make_async_remote_copy(
            src_ref=mine.at[h], dst_ref=gath.at[slot, h], send_sem=gs_sem.at[h, 0], recv_sem=gr_sem.at[h, slot],
            device_id={"ctx": slot + base}, device_id_type=MESH)

    def trecv(slot):
        return pltpu.make_async_remote_copy(
            src_ref=tsend, dst_ref=tgath.at[slot], send_sem=ts_sem.at[0], recv_sem=tr_sem.at[slot],
            device_id={"ctx": slot + base}, device_id_type=MESH)

    def ecopy(h):
        return pltpu.make_async_remote_copy(
            src_ref=eout.at[h], dst_ref=ein.at[h], send_sem=es_sem.at[h], recv_sem=er_sem.at[h],
            device_id={"ctx": ci + group}, device_id_type=MESH)

    def place(j, h):
        return pl.ds(pl.multiple_of((j * heads + h) * HD, HD), HD)

    def ycopy(h, off):
        to = hpeer(off)
        part = pl.ds(pl.multiple_of(to * rows, rows), rows)
        return pltpu.make_async_remote_copy(
            src_ref=u_v.at[part, cols(h)], dst_ref=out_hbm.at[:, place(hi, h)],
            send_sem=ys_sem.at[h, off], recv_sem=yr_sem.at[h, hi],
            device_id={"head": to}, device_id_type=MESH)

    def yrecv(h, j):
        return pltpu.make_async_remote_copy(
            src_ref=u_v.at[pl.ds(0, rows), cols(h)], dst_ref=out_hbm.at[:, place(j, h)],
            send_sem=ys_sem.at[h, 0], recv_sem=yr_sem.at[h, j],
            device_id={"head": j}, device_id_type=MESH)

    def owncopy(h):
        part = pl.ds(pl.multiple_of(hi * rows, rows), rows)
        return pltpu.make_async_copy(u_v.at[part, cols(h)], out_hbm.at[:, place(hi, h)], own_sem.at[h])

    def scopy(off):
        to = hpeer(off)
        return pltpu.make_async_remote_copy(
            src_ref=rows_own.at[to], dst_ref=rows_in.at[hi], send_sem=ss_sem.at[off], recv_sem=sr_sem.at[hi],
            device_id={"head": to}, device_id_type=MESH)

    def srecv(j):
        return pltpu.make_async_remote_copy(
            src_ref=rows_own.at[j], dst_ref=rows_in.at[j], send_sem=ss_sem.at[0], recv_sem=sr_sem.at[j],
            device_id={"head": j}, device_id_type=MESH)

    def states(h):
        load(h, 0).wait()
        load(h, 1).wait()
        state = None
        for s in range(subs):
            span = slice(s * SUB, (s + 1) * SUB)
            col = clc[h, span, :]
            end = dlast[s, pl.ds(h, 1), :]
            keyed = (k_v[span, cols(h)].astype(f32) * jnp.exp(end - col)).astype(bf16)
            new = dot(keyed, v_v[span, cols(h)], ((0,), (0,)))
            sst[h, s] = new
            state = new if state is None else jnp.exp(end) * state + new
        mine[h] = state.astype(bf16)

    def spread_columns(h):
        for s in range(subs):
            span = slice(s * SUB, (s + 1) * SUB)
            clc[h, span, :] = jnp.broadcast_to(tall[s][:, h:h + 1], (SUB, HD))

    def share(h):
        for off in range(1, group):
            gcopy(h, off).start()

    def arrive(h):
        for slot in range(group):
            @pl.when(slot != r)
            def _():
                grecv(h, slot).wait_recv()

    def combine(h):
        arrive(h)
        own = mine[h].astype(f32)
        state = jnp.zeros((HD, HD), f32)
        within = state
        drop = jnp.zeros((1, HD), f32)
        before = drop
        for slot in range(group):
            here = slot == r
            within = jnp.where(here, state, within)
            before = jnp.where(here, drop, before)
            tot = jnp.where(here, tsend[pl.ds(h, 1), :], tgath[slot, pl.ds(h, 1), :])
            part = jnp.where(here, own, gath[slot, h].astype(f32))
            state = jnp.exp(tot) * state + part
            drop = drop + tot

        @pl.when(jnp.logical_not(first))
        def _():
            pltpu.make_async_remote_copy(
                src_ref=eout.at[h], dst_ref=ein.at[h], send_sem=es_sem.at[h], recv_sem=er_sem.at[h],
                device_id={"ctx": ci - group}, device_id_type=MESH).wait_recv()

        enter = jnp.where(first, 0.0, ein[h].astype(f32))
        eout[h] = (jnp.exp(drop) * enter + state).astype(bf16)

        @pl.when(jnp.logical_not(last))
        def _():
            ecopy(h).start()

        return within + jnp.exp(before) * enter

    causal = (
        lax.broadcasted_iota(jnp.int32, (SUB, SUB), 0) >= lax.broadcasted_iota(jnp.int32, (SUB, SUB), 1)
    )

    def attend(h, state):
        load(h, 2).wait()
        load(h, 3).wait()
        gain = gain_ref[pl.ds(hi * heads + h, 1), :]
        for s in range(subs):
            span = slice(s * SUB, (s + 1) * SUB)
            qs = q_v[span, cols(h)]
            col = clc[h, span, :]
            wide = jnp.concatenate([col] * (SUB // HD), axis=1)
            spread = jnp.where(causal, wide - clt[pl.ds(h, 1), span], -1e30)
            scores = dot(qs, k_v[span, cols(h)], ((1,), (1,)))
            weights = (scores * jnp.exp(spread)).astype(bf16)
            inner = dot(weights, v_v[span, cols(h)], ((1,), (0,)))
            across = dot(qs, state.astype(bf16), ((1,), (0,)))
            shade = (inner + jnp.exp(col) * across).astype(bf16).astype(f32)
            acc[span, :] += shade * shade
            gate = g_v[span, cols(h)].astype(f32)
            u_v[span, cols(h)] = (shade * gain * jax.nn.sigmoid(gate)).astype(bf16)
            if s < subs - 1:
                state = jnp.exp(dlast[s, pl.ds(h, 1), :]) * state + sst[h, s]

    spread_columns(0)
    states(0)
    waits = (group - 1) + (n_head - 1) + jnp.where(first, 0, 1) + jnp.where(last, 0, 1)
    pl.semaphore_wait(barrier, waits)
    for off in range(1, group):
        tcopy(off).start()
    share(0)

    def fetch_more(h, _):
        for which in range(4):
            load(h, which).start()
        return 0

    lax.fori_loop(fetch, heads, fetch_more, 0)
    for h in range(1, ahead):
        spread_columns(h)
        states(h)
        share(h)
    for h in range(ahead, heads):
        spread_columns(h)
    for slot in range(group):
        @pl.when(slot != r)
        def _():
            trecv(slot).wait_recv()

    def emit(h):
        state = combine(h)
        attend(h, state)
        for off in range(1, n_head):
            ycopy(h, off).start()
        owncopy(h).start()

    def step(h, _):
        emit(h)
        states(h + ahead)
        share(h + ahead)
        return 0

    def rest(h, _):
        emit(h)
        return 0

    lax.fori_loop(0, heads - ahead, step, 0)
    lax.fori_loop(heads - ahead, heads, rest, 0)

    ones = jnp.ones((8, HD), f32)
    for j in range(n_head):
        rows_own[j] = dot(ones, acc[j * rows:(j + 1) * rows, :], ((1,), (1,)), lax.Precision.HIGHEST)
    for off in range(1, n_head):
        scopy(off).start()

    def finish(h, _):
        for off in range(1, group):
            gcopy(h, off).wait_send()

        @pl.when(jnp.logical_not(last))
        def _():
            ecopy(h).wait_send()

        for off in range(1, n_head):
            ycopy(h, off).wait_send()
        owncopy(h).wait()
        for j in range(n_head):
            @pl.when(j != hi)
            def _():
                yrecv(h, j).wait_recv()
        return 0

    lax.fori_loop(0, heads, finish, 0)
    for off in range(1, group):
        tcopy(off).wait_send()
    for off in range(1, n_head):
        scopy(off).wait_send()
    for j in range(n_head):
        @pl.when(j != hi)
        def _():
            srecv(j).wait_recv()
    total = rows_own[hi]
    for j in range(n_head):
        total = total + jnp.where(j == hi, 0.0, rows_in[j])
    ssq_ref[...] = total


def body(n_ctx, n_head, queries, keys, values, log_decay, gate, norm_gain):
    count, heads = log_decay.shape
    width = queries.shape[1]
    columns = width * n_head
    rows = count // n_head
    group = 4 if n_ctx % 4 == 0 else 1
    subs = count // SUB
    gain = norm_gain.reshape(n_head * heads, HD)
    dma = pltpu.SemaphoreType.DMA
    whole = lambda dtype: pltpu.VMEM((count, width), dtype)
    anywhere = pl.BlockSpec(memory_space=pl.ANY)
    vmem = pl.BlockSpec(memory_space=pltpu.VMEM)
    out, ssq = pl.pallas_call(
        functools.partial(kernel, n_ctx, n_head, group, heads, min(2, heads), min(4, heads)),
        out_shape=(
            jax.ShapeDtypeStruct((rows, columns), bf16),
            jax.ShapeDtypeStruct((8, rows), f32),
        ),
        in_specs=[anywhere] * 4 + [vmem] * 2,
        out_specs=(anywhere, vmem),
        scratch_shapes=[
            whole(bf16), whole(bf16), whole(bf16), whole(bf16), whole(bf16),
            pltpu.VMEM((heads, count), f32),
            pltpu.VMEM((heads, count, HD), f32),
            pltpu.VMEM((subs, heads, HD), f32),
            pltpu.VMEM((heads, subs, HD, HD), f32),
            pltpu.VMEM((heads, HD, HD), bf16),
            pltpu.VMEM((group, heads, HD, HD), bf16),
            pltpu.VMEM((heads, HD), f32),
            pltpu.VMEM((group, heads, HD), f32),
            pltpu.VMEM((heads, HD, HD), bf16),
            pltpu.VMEM((heads, HD, HD), bf16),
            pltpu.VMEM((count, HD), f32),
            pltpu.VMEM((n_head, 8, rows), f32),
            pltpu.VMEM((n_head, 8, rows), f32),
            dma((4, heads)),
            dma((heads, group)), dma((heads, group)),
            dma((group,)), dma((group,)),
            dma((heads,)), dma((heads,)),
            dma((heads, n_head)), dma((heads, n_head)),
            dma((heads,)),
            dma((n_head,)), dma((n_head,)),
        ],
        compiler_params=pltpu.CompilerParams(
            collective_id=0, has_side_effects=True, vmem_limit_bytes=56 * 1024 * 1024
        ),
        cost_estimate=pl.CostEstimate(
            flops=heads * count * HD * (4 * SUB + 4 * HD),
            bytes_accessed=5 * count * width * 2,
            transcendentals=heads * count * (SUB + 3 * HD),
        ),
    )(queries, keys, values, gate, log_decay.T, gain)
    scale = lax.rsqrt(ssq[0] / columns + eps_norm)[:, None]
    return (out.astype(f32) * scale).astype(bf16)


def solution(mesh):
    spec = P("ctx", "head")
    return jax.shard_map(
        functools.partial(body, mesh.shape["ctx"], mesh.shape["head"]),
        mesh=mesh,
        in_specs=(spec, spec, spec, spec, spec, P()),
        out_specs=P(("ctx", "head"), None),
        check_vma=False,
    )
```

time: 416 us -> 70.9 us (0.17); the launches traced: 408 us -> 70.6 us
  waiting for transfers between devices: 108 us -> 0 us
  matrix products: 102 us -> 0 us
  blocking collectives: 72 us -> 0 us
  local copies, waits for them, and re-layouts: 69.8 us -> 0 us
  Pallas kernels: 0 us -> 64.2 us
  other arithmetic: 41.7 us -> 6.38 us
  between operations: 13.5 us -> 0.01 us
    all_gather x1 -> x0, waiting for transfers between devices: 108 us -> none  [carried_in(): pieces = jax.tree.map(lambda part: lax.all_gather(part, axis), value)]
    dot_general x33 -> x0, matrix products: 102 us -> none  [the longest x16 53 us: head_block(): inner = jnp.dot(weights, vh, preferred_element_type=jnp.float32)]
    pallas_call x0 -> x1, Pallas kernels: none -> 64.2 us  [body(): pl.pallas_call(functools.partial(kernel, n_ctx, n_head, group, heads, min...]
    all_to_all x1 -> x0, blocking collectives: 50.6 us -> none  [body(): lax.all_to_all(shaped, 'head', split_axis=0, concat_axis=1, tiled=True)]
    select_n x15 -> x0, other arithmetic: 21.9 us -> none  [step(): jnp.where(position < mine, new, old)]
    unnamed x5 -> x0, local copies, waits for them, and re-layouts: 20.1 us -> none
    dynamic_slice x50 -> x0, local copies, waits for them, and re-layouts: 18.4 us -> none  [the longest x48 18.4 us: local_block(): lax.map(lambda parts: head_block(parts[0], parts[1], parts[2], parts[3]),...]
    all_gather x1 -> x0, blocking collectives: 16.5 us -> none  [carried_in(): pieces = jax.tree.map(lambda part: lax.all_gather(part, axis), value)]
  transfers between devices with their start and end apart: 1 -> 0, of which waited for: 1 -> 0; matrix products, arithmetic and copies ran while one was open for 0% -> 0% of each run, Pallas kernels for 0% -> 0%
where the time goes in v1:
time: 70.9 us; the launch traced here: 70.6 us
  Pallas kernels  64.2 us (91%)
  other arithmetic  6.38 us (9%)
    pallas_call x1, Pallas kernels, body(): pl.pallas_call(functools.partial(kernel, n_ctx, n_head, group, heads, min...  64.2 us
    convert_element_type x1, other arithmetic, body(): return (out.astype(f32) * scale).astype(bf16)  5.65 us

profile of v1, /device:TPU:26, one launch (start us, length us, event | category | flops | bytes accessed | tf_op | source)
XLA Modules:
  0.0 70.6 jit_solution(4360931198646936538)
XLA Ops:
  0.0 64.2 %shard_map.64 = (bf16[512,4096]{1,0:T(8,128)(2,1)}, f32[8,512]{1,0:T(8,128)}) custom-call(bf16[1024,2048]{1,0:T(8,128)(2,1)} %q_hbm.1, bf16[1024,2048]{1,0:T(8,128)(2,1)} %k_hbm.1, bf16[1024,2048]{1,0:T(8,128)(2,1)} %v_hbm.1, bf16[1024,2048]{1,0:T(8,128)(2,1)} %g_hbm.1, f32[16,1024]{1,0:T(8,128)} %bitcast.4, f32[32,128]{1,0:T(8,128)} %bitcast.5), custom_call_target="tpu_custom_call" | custom-call | flops 3221225472 | bytes 20971520 | tf_op jit(solution)/shard_map/pallas_call | solution.py:331
  64.2 0.7 %add_rsqrt_fusion = f32[1,512]{1,0:T(1,128)S(1)} fusion(f32[8,512]{1,0:T(8,128)} %get-tuple-element.8), kind=kLoop, calls=%fused_computation.1 | loop fusion | flops 1024 | bytes 4096 | tf_op jit(solution)/shard_map/rsqrt | solution.py:371
  64.9 5.7 %multiply_convert_fusion = bf16[512,4096]{1,0:T(8,128)(2,1)} fusion(bf16[512,4096]{1,0:T(8,128)(2,1)} %get-tuple-element.7, f32[512]{0:T(512)S(1)} %bitcast.3), kind=kLoop, calls=%fused_computation | loop fusion | flops 6291456 | bytes 8390656 | tf_op jit(solution)/shard_map/convert_element_type | solution.py:372

commit v2 on v1

--- a/solution.py
+++ b/solution.py
@@ -70,21 +70,16 @@
         return pltpu.make_async_copy(src.at[:, cols(h)], dst.at[:, cols(h)], load_sem.at[which, h])
 
     for h in range(fetch):
-        load(h, 0).start()
-        load(h, 1).start()
-    for h in range(fetch):
-        load(h, 2).start()
-        load(h, 3).start()
+        for which in range(4):
+            load(h, which).start()
 
     up = (
         lax.broadcasted_iota(jnp.int32, (SUB, SUB), 0) <= lax.broadcasted_iota(jnp.int32, (SUB, SUB), 1)
     ).astype(f32)
     total = jnp.zeros((heads, 1), f32)
-    tall = []
     for s in range(subs):
         cl = dot(ld_ref[:, s * SUB:(s + 1) * SUB], up, ((1,), (0,)), lax.Precision.HIGHEST)
         clt[:, s * SUB:(s + 1) * SUB] = cl
-        tall.append(jnp.transpose(cl))
         end = cl[:, SUB - 1:SUB]
         dlast[s] = jnp.broadcast_to(end, (heads, HD))
         total = total + end
@@ -117,25 +112,25 @@
             device_id={"ctx": ci + group}, device_id_type=MESH)
 
     def place(j, h):
-        return pl.ds(pl.multiple_of((j * heads + h) * HD, HD), HD)
+        return j * heads + h
 
     def ycopy(h, off):
         to = hpeer(off)
         part = pl.ds(pl.multiple_of(to * rows, rows), rows)
         return pltpu.make_async_remote_copy(
-            src_ref=u_v.at[part, cols(h)], dst_ref=out_hbm.at[:, place(hi, h)],
+            src_ref=u_v.at[h, part], dst_ref=out_hbm.at[place(hi, h)],
             send_sem=ys_sem.at[h, off], recv_sem=yr_sem.at[h, hi],
             device_id={"head": to}, device_id_type=MESH)
 
     def yrecv(h, j):
         return pltpu.make_async_remote_copy(
-            src_ref=u_v.at[pl.ds(0, rows), cols(h)], dst_ref=out_hbm.at[:, place(j, h)],
+            src_ref=u_v.at[h, pl.ds(0, rows)], dst_ref=out_hbm.at[place(j, h)],
             send_sem=ys_sem.at[h, 0], recv_sem=yr_sem.at[h, j],
             device_id={"head": j}, device_id_type=MESH)
 
     def owncopy(h):
         part = pl.ds(pl.multiple_of(hi * rows, rows), rows)
-        return pltpu.make_async_copy(u_v.at[part, cols(h)], out_hbm.at[:, place(hi, h)], own_sem.at[h])
+        return pltpu.make_async_copy(u_v.at[h, part], out_hbm.at[place(hi, h)], own_sem.at[h])
 
     def scopy(off):
         to = hpeer(off)
@@ -154,18 +149,15 @@
         state = None
         for s in range(subs):
             span = slice(s * SUB, (s + 1) * SUB)
-            col = clc[h, span, :]
+            row = clt[pl.ds(h, 1), span]
+            col = jnp.transpose(jnp.broadcast_to(row, (HD, SUB)))
+            clc[h, span, :] = col
             end = dlast[s, pl.ds(h, 1), :]
             keyed = (k_v[span, cols(h)].astype(f32) * jnp.exp(end - col)).astype(bf16)
             new = dot(keyed, v_v[span, cols(h)], ((0,), (0,)))
             sst[h, s] = new
             state = new if state is None else jnp.exp(end) * state + new
         mine[h] = state.astype(bf16)
-
-    def spread_columns(h):
-        for s in range(subs):
-            span = slice(s * SUB, (s + 1) * SUB)
-            clc[h, span, :] = jnp.broadcast_to(tall[s][:, h:h + 1], (SUB, HD))
 
     def share(h):
         for off in range(1, group):
@@ -229,11 +221,11 @@
             shade = (inner + jnp.exp(col) * across).astype(bf16).astype(f32)
             acc[span, :] += shade * shade
             gate = g_v[span, cols(h)].astype(f32)
-            u_v[span, cols(h)] = (shade * gain * jax.nn.sigmoid(gate)).astype(bf16)
+            opened = 0.5 * jnp.tanh(0.5 * gate) + 0.5
+            u_v[h, span, :] = (shade * gain * opened).astype(bf16)
             if s < subs - 1:
                 state = jnp.exp(dlast[s, pl.ds(h, 1), :]) * state + sst[h, s]
 
-    spread_columns(0)
     states(0)
     waits = (group - 1) + (n_head - 1) + jnp.where(first, 0, 1) + jnp.where(last, 0, 1)
     pl.semaphore_wait(barrier, waits)
@@ -241,18 +233,9 @@
         tcopy(off).start()
     share(0)
 
-    def fetch_more(h, _):
-        for which in range(4):
-            load(h, which).start()
-        return 0
-
-    lax.fori_loop(fetch, heads, fetch_more, 0)
     for h in range(1, ahead):
-        spread_columns(h)
         states(h)
         share(h)
-    for h in range(ahead, heads):
-        spread_columns(h)
     for slot in range(group):
         @pl.when(slot != r)
         def _():
@@ -266,16 +249,25 @@
         owncopy(h).start()
 
     def step(h, _):
+        for which in range(4):
+            load(h + fetch, which).start()
         emit(h)
         states(h + ahead)
         share(h + ahead)
         return 0
 
+    def later(h, _):
+        emit(h)
+        states(h + ahead)
+        share(h + ahead)
+        return 0
+
     def rest(h, _):
         emit(h)
         return 0
 
-    lax.fori_loop(0, heads - ahead, step, 0)
+    lax.fori_loop(0, heads - fetch, step, 0)
+    lax.fori_loop(heads - fetch, heads - ahead, later, 0)
     lax.fori_loop(heads - ahead, heads, rest, 0)
 
     ones = jnp.ones((8, HD), f32)
@@ -314,6 +306,14 @@
     for j in range(n_head):
         total = total + jnp.where(j == hi, 0.0, rows_in[j])
     ssq_ref[...] = total
+
+
+def rescale(columns, u_ref, ssq_ref, o_ref):
+    block = o_ref.shape[0]
+    row = lax.rsqrt(ssq_ref[0:1, :] / columns + eps_norm)
+    scale = jnp.transpose(jnp.broadcast_to(row, (HD, block)))
+    for h in range(u_ref.shape[0]):
+        o_ref[:, h * HD:(h + 1) * HD] = (u_ref[h].astype(f32) * scale).astype(bf16)
 
 
 def body(n_ctx, n_head, queries, keys, values, log_decay, gate, norm_gain):
@@ -329,15 +329,16 @@
     anywhere = pl.BlockSpec(memory_space=pl.ANY)
     vmem = pl.BlockSpec(memory_space=pltpu.VMEM)
     out, ssq = pl.pallas_call(
-        functools.partial(kernel, n_ctx, n_head, group, heads, min(2, heads), min(4, heads)),
+        functools.partial(kernel, n_ctx, n_head, group, heads, min(2, heads), min(3, heads)),
         out_shape=(
-            jax.ShapeDtypeStruct((rows, columns), bf16),
+            jax.ShapeDtypeStruct((n_head * heads, rows, HD), bf16),
             jax.ShapeDtypeStruct((8, rows), f32),
         ),
         in_specs=[anywhere] * 4 + [vmem] * 2,
         out_specs=(anywhere, vmem),
         scratch_shapes=[
-            whole(bf16), whole(bf16), whole(bf16), whole(bf16), whole(bf16),
+            whole(bf16), whole(bf16), whole(bf16), whole(bf16),
+            pltpu.VMEM((heads, count, HD), bf16),
             pltpu.VMEM((heads, count), f32),
             pltpu.VMEM((heads, count, HD), f32),
             pltpu.VMEM((subs, heads, HD), f32),
@@ -360,7 +361,7 @@
             dma((n_head,)), dma((n_head,)),
         ],
         compiler_params=pltpu.CompilerParams(
-            collective_id=0, has_side_effects=True, vmem_limit_bytes=56 * 1024 * 1024
+            collective_id=0, has_side_effects=True, vmem_limit_bytes=46 * 1024 * 1024
         ),
         cost_estimate=pl.CostEstimate(
             flops=heads * count * HD * (4 * SUB + 4 * HD),
@@ -368,8 +369,21 @@
             transcendentals=heads * count * (SUB + 3 * HD),
         ),
     )(queries, keys, values, gate, log_decay.T, gain)
-    scale = lax.rsqrt(ssq[0] / columns + eps_norm)[:, None]
-    return (out.astype(f32) * scale).astype(bf16)
+    block = min(128, rows)
+    total_heads = n_head * heads
+    return pl.pallas_call(
+        functools.partial(rescale, columns),
+        grid=(rows // block,),
+        out_shape=jax.ShapeDtypeStruct((rows, columns), bf16),
+        in_specs=[
+            pl.BlockSpec((total_heads, block, HD), lambda i: (0, i, 0)),
+            pl.BlockSpec((8, block), lambda i: (0, i)),
+        ],
+        out_specs=pl.BlockSpec((block, columns), lambda i: (i, 0)),
+        compiler_params=pltpu.CompilerParams(vmem_limit_bytes=16 * 1024 * 1024),
+        cost_estimate=pl.CostEstimate(
+            flops=rows * columns, bytes_accessed=4 * rows * columns, transcendentals=rows),
+    )(out, ssq)
 
 
 def solution(mesh):

time: 70.9 us -> 68.2 us (0.962)
  other arithmetic: 6.38 us -> 0 us
  Pallas kernels: 64.2 us -> 66.3 us
  local copies, waits for them, and re-layouts: 0 us -> 1.56 us
    convert_element_type x1 -> x0, other arithmetic: 5.65 us -> none  [body(): return (out.astype(f32) * scale).astype(bf16)]
    pallas_call x0 -> x1, Pallas kernels: none -> 3.2 us  [body(): pl.pallas_call(functools.partial(rescale, columns), grid=(rows // block,)...]
    unnamed x0 -> x4, local copies, waits for them, and re-layouts: none -> 1.56 us
    pallas_call x1, Pallas kernels: 64.2 us -> 63.1 us  [body(): pl.pallas_call(functools.partial(kernel, n_ctx, n_head, group, heads, min...]
    rsqrt x1 -> x0, other arithmetic: 0.73 us -> none  [body(): scale = lax.rsqrt(ssq[0] / columns + eps_norm)[:, None]]
where the time goes in v2:
time: 68.2 us; the launch traced here: 67.9 us
  Pallas kernels  66.3 us (97%)
  local copies, waits for them, and re-layouts  1.56 us (2%)
    pallas_call x1, Pallas kernels, body(): pl.pallas_call(functools.partial(kernel, n_ctx, n_head, group, heads, min...  63.1 us
    pallas_call x1, Pallas kernels, body(): pl.pallas_call(functools.partial(rescale, columns), grid=(rows // block,)...  3.2 us
    unnamed x4, local copies, waits for them, and re-layouts  1.56 us

profile of v2, /device:TPU:26, one launch (start us, length us, event | category | flops | bytes accessed | tf_op | source)
XLA Modules:
  0.0 67.9 jit_solution(12154026368547629390)
XLA Ops:
  0.0 0.0 copy-start
  0.0 0.8 %copy-done = f32[1024,16]{0,1:T(8,128)S(1)} copy-done((f32[1024,16]{0,1:T(8,128)S(1)}, f32[1024,16]{0,1:T(8,128)}, u32[]{:S(2)}) %copy-start) | copy-done | bytes 65560
  0.8 0.0 copy-start.1
  0.8 0.7 %copy-done.1 = f32[4096]{0:T(1024)S(1)} copy-done((f32[4096]{0:T(1024)S(1)}, f32[4096]{0:T(1024)}, u32[]{:S(2)}) %copy-start.1) | copy-done | bytes 16408
  1.6 63.1 %shard_map.64 = (bf16[32,512,128]{2,1,0:T(8,128)(2,1)S(1)}, f32[8,512]{1,0:T(8,128)S(1)}) custom-call(bf16[1024,2048]{1,0:T(8,128)(2,1)} %q_hbm.1, bf16[1024,2048]{1,0:T(8,128)(2,1)} %k_hbm.1, bf16[1024,2048]{1,0:T(8,128)(2,1)} %v_hbm.1, bf16[1024,2048]{1,0:T(8,128)(2,1)} %g_hbm.1, f32[16,1024]{1,0:T(8,128)S(1)} %bitcast.2, f32[32,128]{1,0:T(8,128)S(1)} %bitcast.3), custom_call_target="tpu_custom_call" | custom-call | flops 3221225472 | bytes 20971520 | tf_op jit(solution)/shard_map/pallas_call | solution.py:331
  64.7 3.2 %shard_map.65 = bf16[512,4096]{1,0:T(8,128)(2,1)} custom-call(bf16[32,512,128]{2,1,0:T(8,128)(2,1)S(1)} %get-tuple-element.7.u_ref, f32[8,512]{1,0:T(8,128)S(1)} %get-tuple-element.8.ssq_ref), custom_call_target="tpu_custom_call" | custom-call | flops 2097152 | bytes 8388608 | tf_op jit(solution)/shard_map/pallas_call | solution.py:374
Async XLA Ops:
  0.0 0.8 %copy-start = (f32[1024,16]{0,1:T(8,128)S(1)}, f32[1024,16]{0,1:T(8,128)}, u32[]{:S(2)}) copy-start(f32[1024,16]{0,1:T(8,128)} %param.9) | copy-start | bytes 196612
  0.8 0.7 %copy-start.1 = (f32[4096]{0:T(1024)S(1)}, f32[4096]{0:T(1024)}, u32[]{:S(2)}) copy-start(f32[4096]{0:T(1024)} %param.11) | copy-start | bytes 49156

commit v3 on v2

--- a/solution.py
+++ b/solution.py
@@ -21,12 +21,13 @@
 
 def kernel(
     n_ctx, n_head, group, heads, ahead, fetch,
-    q_hbm, k_hbm, v_hbm, g_hbm, ld_ref, gain_ref,
-    out_hbm, ssq_ref,
-    q_v, k_v, v_v, g_v, u_v, clt, clc, dlast, sst, mine, gath, tsend, tgath, ein, eout, acc, rows_own, rows_in,
+    q_hbm, k_hbm, v_hbm, g_hbm, ld_ref,
+    out_hbm, scale_ref,
+    inn, q_v, k_v, v_v, g_v, u_v, clt, clc, dlast, sst, mine, gath, tsend, tgath, ein, eout, acc, rows_own, rows_in,
     load_sem, gs_sem, gr_sem, ts_sem, tr_sem, es_sem, er_sem, ys_sem, yr_sem, own_sem, ss_sem, sr_sem,
 ):
     count = ld_ref.shape[1]
+    columns = n_head * heads * HD
     subs = count // SUB
     rows = count // n_head
     planes = n_ctx // group
@@ -72,19 +73,28 @@
     for h in range(fetch):
         for which in range(4):
             load(h, which).start()
+    acc[...] = jnp.zeros_like(acc)
 
     up = (
         lax.broadcasted_iota(jnp.int32, (SUB, SUB), 0) <= lax.broadcasted_iota(jnp.int32, (SUB, SUB), 1)
-    ).astype(f32)
+    ).astype(f32).astype(bf16)
+    parts = []
+    for s in range(subs):
+        left = ld_ref[:, s * SUB:(s + 1) * SUB]
+        for _ in range(3):
+            part = left.astype(bf16).astype(f32)
+            parts.append(part)
+            left = left - part
+    sums = dot(jnp.concatenate(parts, axis=0).astype(bf16), up, ((1,), (0,)))
     total = jnp.zeros((heads, 1), f32)
     for s in range(subs):
-        cl = dot(ld_ref[:, s * SUB:(s + 1) * SUB], up, ((1,), (0,)), lax.Precision.HIGHEST)
+        at = 3 * s * heads
+        cl = (sums[at + 2 * heads:at + 3 * heads] + sums[at + heads:at + 2 * heads]) + sums[at:at + heads]
         clt[:, s * SUB:(s + 1) * SUB] = cl
         end = cl[:, SUB - 1:SUB]
         dlast[s] = jnp.broadcast_to(end, (heads, HD))
         total = total + end
     tsend[...] = jnp.broadcast_to(total, (heads, HD))
-    acc[...] = jnp.zeros_like(acc)
 
     def tcopy(off):
         return pltpu.make_async_remote_copy(
@@ -204,25 +214,27 @@
         lax.broadcasted_iota(jnp.int32, (SUB, SUB), 0) >= lax.broadcasted_iota(jnp.int32, (SUB, SUB), 1)
     )
 
-    def attend(h, state):
-        load(h, 2).wait()
+    def diagonal(h, s):
+        span = slice(s * SUB, (s + 1) * SUB)
+        wide = jnp.concatenate([clc[h, span, :]] * (SUB // HD), axis=1)
+        spread = jnp.where(causal, wide - clt[pl.ds(h, 1), span], -1e30)
+        scores = dot(q_v[span, cols(h)], k_v[span, cols(h)], ((1,), (1,)))
+        weights = (scores * jnp.exp(spread)).astype(bf16)
+        return dot(weights, v_v[span, cols(h)], ((1,), (0,)))
+
+    def attend(h, state, ready):
+        if not ready:
+            load(h, 2).wait()
         load(h, 3).wait()
-        gain = gain_ref[pl.ds(hi * heads + h, 1), :]
         for s in range(subs):
             span = slice(s * SUB, (s + 1) * SUB)
-            qs = q_v[span, cols(h)]
-            col = clc[h, span, :]
-            wide = jnp.concatenate([col] * (SUB // HD), axis=1)
-            spread = jnp.where(causal, wide - clt[pl.ds(h, 1), span], -1e30)
-            scores = dot(qs, k_v[span, cols(h)], ((1,), (1,)))
-            weights = (scores * jnp.exp(spread)).astype(bf16)
-            inner = dot(weights, v_v[span, cols(h)], ((1,), (0,)))
-            across = dot(qs, state.astype(bf16), ((1,), (0,)))
-            shade = (inner + jnp.exp(col) * across).astype(bf16).astype(f32)
+            inner = inn[span, :] if ready else diagonal(h, s)
+            across = dot(q_v[span, cols(h)], state.astype(bf16), ((1,), (0,)))
+            shade = (inner + jnp.exp(clc[h, span, :]) * across).astype(bf16).astype(f32)
             acc[span, :] += shade * shade
             gate = g_v[span, cols(h)].astype(f32)
             opened = 0.5 * jnp.tanh(0.5 * gate) + 0.5
-            u_v[h, span, :] = (shade * gain * opened).astype(bf16)
+            u_v[h, span, :] = (shade * opened).astype(bf16)
             if s < subs - 1:
                 state = jnp.exp(dlast[s, pl.ds(h, 1), :]) * state + sst[h, s]
 
@@ -236,14 +248,17 @@
     for h in range(1, ahead):
         states(h)
         share(h)
+    load(0, 2).wait()
+    for s in range(subs):
+        inn[s * SUB:(s + 1) * SUB, :] = diagonal(0, s)
     for slot in range(group):
         @pl.when(slot != r)
         def _():
             trecv(slot).wait_recv()
 
-    def emit(h):
+    def emit(h, ready=False):
         state = combine(h)
-        attend(h, state)
+        attend(h, state, ready)
         for off in range(1, n_head):
             ycopy(h, off).start()
         owncopy(h).start()
@@ -266,9 +281,16 @@
         emit(h)
         return 0
 
-    lax.fori_loop(0, heads - fetch, step, 0)
-    lax.fori_loop(heads - fetch, heads - ahead, later, 0)
-    lax.fori_loop(heads - ahead, heads, rest, 0)
+    emit(0, True)
+    if heads > fetch:
+        for which in range(4):
+            load(fetch, which).start()
+    if heads > ahead:
+        states(ahead)
+        share(ahead)
+    lax.fori_loop(1, heads - fetch, step, 0)
+    lax.fori_loop(max(heads - fetch, 1), heads - ahead, later, 0)
+    lax.fori_loop(max(heads - ahead, 1), heads, rest, 0)
 
     ones = jnp.ones((8, HD), f32)
     for j in range(n_head):
@@ -305,15 +327,16 @@
     total = rows_own[hi]
     for j in range(n_head):
         total = total + jnp.where(j == hi, 0.0, rows_in[j])
-    ssq_ref[...] = total
-
-
-def rescale(columns, u_ref, ssq_ref, o_ref):
+    row = lax.rsqrt(total[0:1, :] / columns + eps_norm)
+    scale_ref[...] = jnp.transpose(jnp.broadcast_to(row, (HD, rows)))
+
+
+def rescale(u_ref, scale_ref, gain_ref, o_ref):
     block = o_ref.shape[0]
-    row = lax.rsqrt(ssq_ref[0:1, :] / columns + eps_norm)
-    scale = jnp.transpose(jnp.broadcast_to(row, (HD, block)))
+    part = pl.ds(pl.multiple_of(pl.program_id(0) * block, block), block)
+    scale = scale_ref[part, :]
     for h in range(u_ref.shape[0]):
-        o_ref[:, h * HD:(h + 1) * HD] = (u_ref[h].astype(f32) * scale).astype(bf16)
+        o_ref[:, h * HD:(h + 1) * HD] = (u_ref[h, part, :].astype(f32) * scale * gain_ref[h:h + 1, :]).astype(bf16)
 
 
 def body(n_ctx, n_head, queries, keys, values, log_decay, gate, norm_gain):
@@ -328,15 +351,16 @@
     whole = lambda dtype: pltpu.VMEM((count, width), dtype)
     anywhere = pl.BlockSpec(memory_space=pl.ANY)
     vmem = pl.BlockSpec(memory_space=pltpu.VMEM)
-    out, ssq = pl.pallas_call(
+    out, scale = pl.pallas_call(
         functools.partial(kernel, n_ctx, n_head, group, heads, min(2, heads), min(3, heads)),
         out_shape=(
             jax.ShapeDtypeStruct((n_head * heads, rows, HD), bf16),
-            jax.ShapeDtypeStruct((8, rows), f32),
+            jax.ShapeDtypeStruct((rows, HD), f32),
         ),
-        in_specs=[anywhere] * 4 + [vmem] * 2,
+        in_specs=[anywhere] * 4 + [vmem],
         out_specs=(anywhere, vmem),
         scratch_shapes=[
+            pltpu.VMEM((count, HD), f32),
             whole(bf16), whole(bf16), whole(bf16), whole(bf16),
             pltpu.VMEM((heads, count, HD), bf16),
             pltpu.VMEM((heads, count), f32),
@@ -368,22 +392,18 @@
             bytes_accessed=5 * count * width * 2,
             transcendentals=heads * count * (SUB + 3 * HD),
         ),
-    )(queries, keys, values, gate, log_decay.T, gain)
-    block = min(128, rows)
-    total_heads = n_head * heads
+    )(queries, keys, values, gate, log_decay.T)
+    block = min(64, rows)
     return pl.pallas_call(
-        functools.partial(rescale, columns),
+        rescale,
         grid=(rows // block,),
         out_shape=jax.ShapeDtypeStruct((rows, columns), bf16),
-        in_specs=[
-            pl.BlockSpec((total_heads, block, HD), lambda i: (0, i, 0)),
-            pl.BlockSpec((8, block), lambda i: (0, i)),
-        ],
+        in_specs=[vmem, vmem, vmem],
         out_specs=pl.BlockSpec((block, columns), lambda i: (i, 0)),
         compiler_params=pltpu.CompilerParams(vmem_limit_bytes=16 * 1024 * 1024),
         cost_estimate=pl.CostEstimate(
             flops=rows * columns, bytes_accessed=4 * rows * columns, transcendentals=rows),
-    )(out, ssq)
+    )(out, scale, gain)
 
 
 def solution(mesh):

time: 68.2 us -> 67.9 us (level)
  local copies, waits for them, and re-layouts: 1.56 us -> 0.84 us
    pallas_call x1, Pallas kernels: 3.2 us -> 3.92 us  [body(): pl.pallas_call(rescale, grid=(rows // block,), out_shape=jax.ShapeDtypeSt...]
    unnamed x4, local copies, waits for them, and re-layouts: 1.56 us -> 0.84 us
where the time goes in v3:
time: 67.9 us; the launch traced here: 67.8 us
  Pallas kernels  66.9 us (99%)
  local copies, waits for them, and re-layouts  0.84 us (1%)
    pallas_call x1, Pallas kernels, body(): pl.pallas_call(functools.partial(kernel, n_ctx, n_head, group, heads, min...  63 us
    pallas_call x1, Pallas kernels, body(): pl.pallas_call(rescale, grid=(rows // block,), out_shape=jax.ShapeDtypeSt...  3.92 us

profile of v3, /device:TPU:26, one launch (start us, length us, event | category | flops | bytes accessed | tf_op | source)
XLA Modules:
  0.0 67.8 jit_solution(9235659740927502907)
XLA Ops:
  0.0 0.0 copy-start.1
  0.0 0.8 %copy-done.1 = f32[1024,16]{0,1:T(8,128)S(1)} copy-done((f32[1024,16]{0,1:T(8,128)S(1)}, f32[1024,16]{0,1:T(8,128)}, u32[]{:S(2)}) %copy-start.1) | copy-done | bytes 65560
  0.8 0.0 copy-start
  0.8 63.0 %shard_map.64 = (bf16[32,512,128]{2,1,0:T(8,128)(2,1)S(1)}, f32[512,128]{1,0:T(8,128)S(1)}) custom-call(bf16[1024,2048]{1,0:T(8,128)(2,1)} %q_hbm.1, bf16[1024,2048]{1,0:T(8,128)(2,1)} %k_hbm.1, bf16[1024,2048]{1,0:T(8,128)(2,1)} %v_hbm.1, bf16[1024,2048]{1,0:T(8,128)(2,1)} %g_hbm.1, f32[16,1024]{1,0:T(8,128)S(1)} %bitcast.3), custom_call_target="tpu_custom_call" | custom-call | flops 3221225472 | bytes 20971520 | tf_op jit(solution)/shard_map/pallas_call | solution.py:354
  63.9 0.0 copy-done
  63.9 3.9 %shard_map.65 = bf16[512,4096]{1,0:T(8,128)(2,1)} custom-call(bf16[32,512,128]{2,1,0:T(8,128)(2,1)S(1)} %get-tuple-element.7.u_ref, f32[512,128]{1,0:T(8,128)S(1)} %get-tuple-element.8.scale_ref, f32[32,128]{1,0:T(8,128)S(1)} %bitcast.2), custom_call_target="tpu_custom_call" | custom-call | flops 2097152 | bytes 8388608 | tf_op jit(solution)/shard_map/pallas_call | solution.py:397
Async XLA Ops:
  0.0 0.8 %copy-start.1 = (f32[1024,16]{0,1:T(8,128)S(1)}, f32[1024,16]{0,1:T(8,128)}, u32[]{:S(2)}) copy-start(f32[1024,16]{0,1:T(8,128)} %param.9) | copy-start | bytes 196612
  0.8 63.0 %copy-start = (f32[4096]{0:T(1024)S(1)}, f32[4096]{0:T(1024)}, u32[]{:S(2)}) copy-start(f32[4096]{0:T(1024)} %param.11) | copy-start | bytes 49156

commit v4 on v3

--- a/solution.py
+++ b/solution.py
@@ -332,11 +332,9 @@
 
 
 def rescale(u_ref, scale_ref, gain_ref, o_ref):
-    block = o_ref.shape[0]
-    part = pl.ds(pl.multiple_of(pl.program_id(0) * block, block), block)
-    scale = scale_ref[part, :]
+    scale = scale_ref[...]
     for h in range(u_ref.shape[0]):
-        o_ref[:, h * HD:(h + 1) * HD] = (u_ref[h, part, :].astype(f32) * scale * gain_ref[h:h + 1, :]).astype(bf16)
+        o_ref[:, h * HD:(h + 1) * HD] = (u_ref[h].astype(f32) * scale * gain_ref[h:h + 1, :]).astype(bf16)
 
 
 def body(n_ctx, n_head, queries, keys, values, log_decay, gate, norm_gain):
@@ -393,12 +391,16 @@
             transcendentals=heads * count * (SUB + 3 * HD),
         ),
     )(queries, keys, values, gate, log_decay.T)
-    block = min(64, rows)
+    block = min(128, rows)
     return pl.pallas_call(
         rescale,
         grid=(rows // block,),
         out_shape=jax.ShapeDtypeStruct((rows, columns), bf16),
-        in_specs=[vmem, vmem, vmem],
+        in_specs=[
+            pl.BlockSpec((n_head * heads, block, HD), lambda i: (0, i, 0)),
+            pl.BlockSpec((block, HD), lambda i: (i, 0)),
+            vmem,
+        ],
         out_specs=pl.BlockSpec((block, columns), lambda i: (i, 0)),
         compiler_params=pltpu.CompilerParams(vmem_limit_bytes=16 * 1024 * 1024),
         cost_estimate=pl.CostEstimate(

time: 67.9 us -> 67.2 us (0.990)
  Pallas kernels: 66.9 us -> 66.2 us
    pallas_call x1, Pallas kernels: 3.92 us -> 3.18 us  [body(): pl.pallas_call(rescale, grid=(rows // block,), out_shape=jax.ShapeDtypeSt...]
where the time goes in v4:
time: 67.2 us; the launch traced here: 67 us
  Pallas kernels  66.2 us (99%)
  local copies, waits for them, and re-layouts  0.84 us (1%)
    pallas_call x1, Pallas kernels, body(): pl.pallas_call(functools.partial(kernel, n_ctx, n_head, group, heads, min...  63 us
    pallas_call x1, Pallas kernels, body(): pl.pallas_call(rescale, grid=(rows // block,), out_shape=jax.ShapeDtypeSt...  3.18 us

profile of v4, /device:TPU:26, one launch (start us, length us, event | category | flops | bytes accessed | tf_op | source)
XLA Modules:
  0.0 67.0 jit_solution(4844502072399872896)
XLA Ops:
  0.0 0.0 copy-start.1
  0.0 0.8 %copy-done.1 = f32[1024,16]{0,1:T(8,128)S(1)} copy-done((f32[1024,16]{0,1:T(8,128)S(1)}, f32[1024,16]{0,1:T(8,128)}, u32[]{:S(2)}) %copy-start.1) | copy-done | bytes 65560
  0.8 0.0 copy-start
  0.8 63.0 %shard_map.64 = (bf16[32,512,128]{2,1,0:T(8,128)(2,1)S(1)}, f32[512,128]{1,0:T(8,128)S(1)}) custom-call(bf16[1024,2048]{1,0:T(8,128)(2,1)} %q_hbm.1, bf16[1024,2048]{1,0:T(8,128)(2,1)} %k_hbm.1, bf16[1024,2048]{1,0:T(8,128)(2,1)} %v_hbm.1, bf16[1024,2048]{1,0:T(8,128)(2,1)} %g_hbm.1, f32[16,1024]{1,0:T(8,128)S(1)} %bitcast.3), custom_call_target="tpu_custom_call" | custom-call | flops 3221225472 | bytes 20971520 | tf_op jit(solution)/shard_map/pallas_call | solution.py:352
  63.9 0.0 copy-done
  63.9 3.2 %shard_map.65 = bf16[512,4096]{1,0:T(8,128)(2,1)} custom-call(bf16[32,512,128]{2,1,0:T(8,128)(2,1)S(1)} %get-tuple-element.7.u_ref, f32[512,128]{1,0:T(8,128)S(1)} %get-tuple-element.8.scale_ref, f32[32,128]{1,0:T(8,128)S(1)} %bitcast.2), custom_call_target="tpu_custom_call" | custom-call | flops 2097152 | bytes 8388608 | tf_op jit(solution)/shard_map/pallas_call | solution.py:395
Async XLA Ops:
  0.0 0.8 %copy-start.1 = (f32[1024,16]{0,1:T(8,128)S(1)}, f32[1024,16]{0,1:T(8,128)}, u32[]{:S(2)}) copy-start(f32[1024,16]{0,1:T(8,128)} %param.9) | copy-start | bytes 196612
  0.8 63.0 %copy-start = (f32[4096]{0:T(1024)S(1)}, f32[4096]{0:T(1024)}, u32[]{:S(2)}) copy-start(f32[4096]{0:T(1024)} %param.11) | copy-start | bytes 49156
